TPU v7x, 256 devices: a whole 4x4x8 slice. The times are simulated.
256 devices in a mesh: blk: 64 (over x, z, core), rep: 4 (over y).
Axes of the slice: x: 4, y: 4, z: 8, core: 2. Of those that a mesh axis runs over, the one named last changes fastest.
Arguments:
- right_side: float32 [64, 262144], P(None, 'blk'), may hold values from -6 to 6
- points: float32 [3, 262144], P(None, 'blk'), may hold values from -1 to 544, as said below
- active: int32 [64, 5], replicated, may hold values 0 or 1
Outputs:
- posterior_mean: float32 [64, 262144], P(None, 'blk')
- residual: float32 [64, 262144], P(None, 'blk')
Inputs may be any that keep to these rules, and one draw needn't show every extreme that they name: `points`: point coordinates in lattice units.
All inputs are finite; a program needn't handle non-finite values.
Results may differ from a plain program's by a relative error of at most 0.0003.
Values sent between devices are 32-bit elements; how exact they have to be, the bound alone decides.
No kernel may reach another device: no remote copies, remote signals or barrier semaphores. Data moves between devices by JAX's collectives and lax.ppermute only.
A program may use at most 128 MiB of HBM per device.

v0:
```python
from functools import partial
import jax
import jax.numpy as jnp
from jax import lax
from jax.sharding import PartitionSpec as P

ITERS = 2
B = 2048
support_radius = 2.5
noise_level = 8.0


def from_behind(block, axis, distance):
    devices = range(lax.axis_size(axis))
    route = [(i - distance, i) for i in devices if i - distance in devices]
    return lax.ppermute(block, axis, route)


def wendland(rows, cols):
    delta_x = rows[0][:, None] - cols[0][None, :]
    delta_y = rows[1][:, None] - cols[1][None, :]
    delta_z = rows[2][:, None] - cols[2][None, :]
    scaled = jnp.sqrt(delta_x * delta_x + delta_y * delta_y + delta_z * delta_z) / support_radius
    inside = jnp.maximum(1.0 - scaled, 0.0)
    square = inside * inside
    return square * square * (4.0 * scaled + 1.0)


def apply_rows(vector, kernel_tile):
    return lax.dot_general(
        vector,
        kernel_tile,
        (((1,), (1,)), ((), ())),
        precision=lax.Precision.HIGHEST,
        preferred_element_type=jnp.float32,
    )


def apply_cols(vector, kernel_tile):
    return jnp.dot(
        vector, kernel_tile, precision=lax.Precision.HIGHEST, preferred_element_type=jnp.float32
    )


def pair_flags(active, column, count):
    here = lax.dynamic_slice_in_dim(active, column, 1, 0)[0].astype(jnp.float32)
    before = lax.dynamic_slice_in_dim(active, jnp.maximum(column - 1, 0), 1, 0)[0].astype(
        jnp.float32
    )
    has_before = (column >= 1).astype(jnp.float32)
    has_after = (column + 1 < count).astype(jnp.float32)
    table = []
    for c in range(2):
        entry = []
        for k in range(6):
            if k < 2:
                entry.append(before[1 + 2 * k + c] * has_before)
            elif k == 2 + c:
                entry.append(has_after * 0.0 + 1.0)
            elif k < 4:
                entry.append(here[0])
            else:
                entry.append(here[1 + 2 * c + (k - 4)] * has_after)
        table.append(entry)
    return table


def gated(flag, compute, operands):
    return flag * compute(*operands)


def place_rows(values, start, total):
    return lax.dynamic_update_slice_in_dim(
        jnp.zeros((values.shape[0], total), jnp.float32), values, start, 1
    )


def shards(right_side, points, active):
    count = lax.axis_size("blk")
    column = lax.axis_index("blk")
    groups = lax.axis_size("rep")
    member = lax.axis_index("rep")
    flags = pair_flags(active, column, count)
    rows_each = B // groups
    row_start = member * rows_each
    sides = right_side.shape[0]

    def row_slice(array, c):
        return lax.dynamic_slice_in_dim(array, c * B + row_start, rows_each, 1)

    def fetch(stored, index):
        return stored[index]

    pts_next = from_behind(points, "blk", -1)
    makers = [
        partial(wendland, row_slice(points, c), points[:, c * B : (c + 1) * B]) for c in range(2)
    ]
    makers.append(partial(wendland, row_slice(points, 0), points[:, B : 2 * B]))
    for c in range(2):
        for k in range(2):
            makers.append(partial(wendland, row_slice(points, c), pts_next[:, k * B : (k + 1) * B]))
    stored = [maker() for maker in makers]

    def matvec(vector):
        vec_next = from_behind(vector, "blk", -1)
        own_rows = [row_slice(vector, c) for c in range(2)]
        row_terms = [apply_rows(vector[:, c * B : (c + 1) * B], fetch(stored, c)) for c in range(2)]
        across_tile = fetch(stored, 2)
        row_terms[0] = row_terms[0] + gated(
            flags[0][3], apply_rows, (vector[:, B : 2 * B], across_tile)
        )
        across_back = gated(flags[0][3], apply_cols, (own_rows[0], across_tile))
        next_terms = [jnp.zeros((sides, B), jnp.float32), jnp.zeros((sides, B), jnp.float32)]
        for c in range(2):
            for k in range(2):
                kernel_tile = fetch(stored, 3 + 2 * c + k)
                flag = flags[c][4 + k]
                row_terms[c] = row_terms[c] + gated(
                    flag, apply_rows, (vec_next[:, k * B : (k + 1) * B], kernel_tile)
                )
                next_terms[k] = next_terms[k] + gated(flag, apply_cols, (own_rows[c], kernel_tile))
        own_full = jnp.concatenate(
            [
                place_rows(row_terms[0], row_start, B),
                across_back + place_rows(row_terms[1], row_start, B),
            ],
            axis=1,
        )
        returned = from_behind(jnp.concatenate(next_terms, axis=1), "blk", 1)
        total = lax.psum(own_full + returned, "rep")
        return total + noise_level * vector

    def squares(residual):
        return lax.psum(jnp.sum(residual * residual, axis=1), "blk")

    solution = jnp.zeros_like(right_side)
    residual = right_side
    direction = right_side
    norm_now = squares(residual)
    for step in range(ITERS):
        image = matvec(direction)
        alpha = norm_now / lax.psum(jnp.sum(direction * image, axis=1), "blk")
        solution = solution + alpha[:, None] * direction
        residual = residual - alpha[:, None] * image
        norm_next = squares(residual)
        direction = residual + (norm_next / norm_now)[:, None] * direction
        norm_now = norm_next
    posterior = right_side - noise_level * solution
    return (posterior, residual)


def solution(mesh):
    return jax.shard_map(
        shards,
        mesh=mesh,
        in_specs=(P(None, "blk"), P(None, "blk"), P()),
        out_specs=(P(None, "blk"), P(None, "blk")),
        check_vma=False,
    )
```

profile of v0, /device:TPU:8, one launch (start us, length us, event | category | flops | bytes accessed | tf_op | source)
XLA Modules:
  0.0 681.2 jit_solution(9274392147604572619)
XLA Ops:
  7.2 0.0 all-reduce.4.cloned.1.call-start
  7.2 1.3 collective-permute-start
  8.5 1.3 collective-permute-start.1
  9.8 0.9 fusion.176
  10.7 0.8 dynamic-slice_convert_fusion
  11.5 0.6 fusion.178
  12.1 0.9 constant_dynamic-slice_fusion
  13.1 0.0 copy-start
  13.1 8.3 %fusion.17 = f32[512,64]{0,1:T(8,128)S(1)} fusion(f32[512]{0:T(512)S(1)} %bitcast.125, f32[512]{0:T(512)S(1)} %bitcast.115, f32[512]{0:T(512)S(1)} %bitcast.105, f32[2048]{0:T(1024)S(1)} %bitcast.39, f32[2048]{0:T(1024)S(1)} %bitcast.45, f32[2048]{0:T(1024)S(1)} %bitcast.51, f32[64,4096]{1,0:T(8,128)} %param.3), kind=kOutput, calls=%fused_computation.34 | convolution fusion | flops 822083584 | bytes 686080 | tf_op jit(solution)/shard_map/dot_general | solution.py:30
  21.4 0.0 copy-done
  21.4 8.1 %fusion.44 = f32[512,64]{0,1:T(8,128)S(1)} fusion(f32[2048]{0:T(1024)S(1)} %bitcast.40, f32[2048]{0:T(1024)S(1)} %bitcast.46, f32[2048]{0:T(1024)S(1)} %bitcast.52, f32[512]{0:T(512)S(1)} %bitcast.163, f32[512]{0:T(512)S(1)} %bitcast.135, f32[512]{0:T(512)S(1)} %bitcast.149, f32[64,4096]{1,0:T(8,128)S(1)} %copy-done, f32[]{:T(128)} %bitcast.6), kind=kOutput, calls=%fused_computation.61 | convolution fusion | flops 822116352 | bytes 686084 | tf_op jit(solution)/shard_map/dot_general | solution.py:30
  29.5 7.2 %fusion.18 = f32[512,64]{0,1:T(8,128)S(1)} fusion(f32[512,64]{0,1:T(8,128)S(1)} %fusion.44, f32[2048]{0:T(1024)S(1)} %bitcast.35, f32[512]{0:T(512)S(1)} %bitcast.164, f32[2048]{0:T(1024)S(1)} %bitcast.37, f32[512]{0:T(512)S(1)} %bitcast.136, f32[2048]{0:T(1024)S(1)} %bitcast.33, f32[512]{0:T(512)S(1)} %bitcast.150, f32[64,4096]{1,0:T(8,128)S(1)} %copy-done), kind=kOutput, calls=%fused_computation.35 | convolution fusion | flops 822116352 | bytes 817152 | tf_op jit(solution)/shard_map/dot_general | solution.py:30
  36.7 6.6 convolution_multiply_fusion.9
  45.7 0.0 collective-permute-done
  45.8 5.7 convolution_multiply_fusion.8
  51.6 5.7 fusion.3
  57.3 5.9 convolution_multiply_fusion.6
  63.3 5.7 fusion.2
  69.0 0.1 pad_maximum_fusion
  69.1 4.1 collective-permute-start.2
  73.2 0.0 collective-permute-done.1
  73.2 7.2 %fusion.41 = f32[512,64]{0,1:T(8,128)S(1)} fusion(f32[512,64]{0,1:T(8,128)S(1)} %fusion.18, f32[2048]{0:T(1024)S(1)} %bitcast.91, f32[2048]{0:T(1024)S(1)} %bitcast.99, f32[2048]{0:T(1024)S(1)} %bitcast.83, f32[512]{0:T(512)S(1)} %bitcast.168, f32[512]{0:T(512)S(1)} %bitcast.140, f32[512]{0:T(512)S(1)} %bitcast.154, ...), kind=kOutput, calls=%fused_computation.58 | convolution fusion | flops 822149120 | bytes 817156 | tf_op jit(solution)/shard_map/dot_general | solution.py:30
  80.4 7.3 %fusion.36 = f32[64,2048]{1,0:T(8,128)S(1)} fusion(f32[64,2048]{1,0:T(8,128)S(1)} %broadcast.47.clone, s32[]{:T(128)S(6)} %select_n.10, f32[512,64]{0,1:T(8,128)S(1)} %fusion.41, f32[2048]{0:T(1024)S(1)} %bitcast.59, f32[2048]{0:T(1024)S(1)} %bitcast.67, f32[2048]{0:T(1024)S(1)} %bitcast.75, f32[512]{0:T(512)S(1)} %bitcast.169, f32[512]{0:T(512)S(1)} %bitcast.141, ...), kind=kOutput, calls=%fused_computation.53 | convolution fusion | flops 822149120 | bytes 817160 | tf_op jit(solution)/shard_map/dot_general | solution.py:30
  87.8 7.2 %fusion.30 = f32[512,64]{0,1:T(8,128)S(1)} fusion(f32[512,64]{0,1:T(8,128)S(1)} %fusion.17, f32[512]{0:T(512)S(1)} %bitcast.128, f32[512]{0:T(512)S(1)} %bitcast.118, f32[512]{0:T(512)S(1)} %bitcast.108, f32[2048]{0:T(1024)S(1)} %bitcast.92, f32[2048]{0:T(1024)S(1)} %bitcast.100, f32[2048]{0:T(1024)S(1)} %bitcast.84, ...), kind=kOutput, calls=%fused_computation.47 | convolution fusion | flops 822149120 | bytes 817156 | tf_op jit(solution)/shard_map/dot_general | solution.py:30
  95.0 7.4 %fusion.24 = f32[64,2048]{1,0:T(8,128)S(1)} fusion(f32[64,2048]{1,0:T(8,128)S(1)} %convolution_multiply_fusion.9, s32[]{:T(128)S(6)} %select_n.10, f32[512,64]{0,1:T(8,128)S(1)} %fusion.30, f32[512]{0:T(512)S(1)} %bitcast.129, f32[512]{0:T(512)S(1)} %bitcast.119, f32[512]{0:T(512)S(1)} %bitcast.109, f32[2048]{0:T(1024)S(1)} %bitcast.60, ...), kind=kOutput, calls=%fused_computation.41 | convolution fusion | flops 822181888 | bytes 948232 | tf_op jit(solution)/shard_map/dot_general | solution.py:30
  102.3 0.0 collective-permute-done.2
  102.3 1.1 maximum_add_fusion
  103.4 0.0 all-reduce.4.cloned.1.call-update
  103.5 0.0 all-reduce.6.cloned.1.call-start
  103.5 55.2 %all-reduce.4.cloned.1.call-done = f32[64,4096]{1,0:T(8,128)} async-done(((f32[64,4096]{1,0:T(8,128)}), f32[64,4096]{1,0:T(8,128)}) %all-reduce.4.cloned.1.call-update) | async-done | bytes 1048592 | tf_op jit(solution)/shard_map/psum | solution.py:130
  158.7 0.0 copy-start.1
  158.7 1.6 multiply_reduce_fusion.2
  160.4 127.9 %all-reduce = (f32[64]{0:T(128)S(1)}, f32[64]{0:T(128)S(1)}) all-reduce(f32[64]{0:T(128)S(1)} %get-tuple-element.3, f32[64]{0:T(128)S(1)} %get-tuple-element.2), channel_id=1, replica_groups=mesh['blk'=64,'rep'=4] {'blk'}, use_global_device_ids=true, to_apply=%region_1.0 | all-reduce | flops 128 | bytes 1024 | tf_op jit(solution)/shard_map/psum | solution.py:134
  288.3 0.0 copy-done.1
  288.3 0.3 multiply_reduce_fusion.1
  288.6 124.1 %psum.45 = f32[64]{0:T(128)S(1)} all-reduce(f32[64]{0:T(128)S(1)} %multiply_reduce_fusion.1), channel_id=1, replica_groups=mesh['blk'=64,'rep'=4] {'blk'}, use_global_device_ids=true, to_apply=%region_6.0 | all-reduce | flops 64 | bytes 512 | tf_op jit(solution)/shard_map/psum | solution.py:134
  412.7 0.3 multiply_add_fusion.1
  412.9 7.4 %fusion.45 = f32[64,512]{1,0:T(8,128)S(1)} fusion(f32[2048]{0:T(1024)S(1)} %bitcast.42, f32[2048]{0:T(1024)S(1)} %bitcast.48, f32[2048]{0:T(1024)S(1)} %bitcast.54, f32[512]{0:T(512)S(1)} %bitcast.170, f32[512]{0:T(512)S(1)} %bitcast.142, f32[512]{0:T(512)S(1)} %bitcast.156, f32[64,4096]{1,0:T(8,128)S(1)} %multiply_add_fusion.1, f32[]{:T(128)} %bitcast.6), kind=kOutput, calls=%fused_computation.62 | convolution fusion | flops 822116352 | bytes 686084 | tf_op jit(solution)/shard_map/dot_general | solution.py:30
  420.3 1.7 collective-permute-start.3
  422.0 6.7 fusion.16
  428.8 5.7 convolution_multiply_fusion.3
  434.5 5.9 convolution_multiply_fusion.1
  440.4 5.7 fusion.1
  446.2 6.1 fusion
  452.3 0.1 pad_maximum_fusion.1
  452.4 3.1 collective-permute-start.4
  455.5 6.4 convolution_multiply_fusion.4
  461.9 6.7 fusion.19
  468.6 0.0 collective-permute-done.3
  468.7 6.9 %fusion.43 = f32[64,512]{1,0:T(8,128)S(1)} fusion(f32[64,512]{1,0:T(8,128)S(1)} %fusion.19, f32[2048]{0:T(1024)S(1)} %bitcast.95, f32[2048]{0:T(1024)S(1)} %bitcast.103, f32[2048]{0:T(1024)S(1)} %bitcast.87, f32[512]{0:T(512)S(1)} %bitcast.175, f32[512]{0:T(512)S(1)} %bitcast.147, f32[512]{0:T(512)S(1)} %bitcast.161, ...), kind=kOutput, calls=%fused_computation.60 | convolution fusion | flops 822149120 | bytes 817156 | tf_op jit(solution)/shard_map/dot_general | solution.py:30
  475.6 6.8 fusion.39
  482.4 7.0 %fusion.32 = f32[64,512]{1,0:T(8,128)S(1)} fusion(f32[64,512]{1,0:T(8,128)S(1)} %fusion.16, f32[512]{0:T(512)S(1)} %bitcast.133, f32[512]{0:T(512)S(1)} %bitcast.123, f32[512]{0:T(512)S(1)} %bitcast.113, f32[2048]{0:T(1024)S(1)} %bitcast.96, f32[2048]{0:T(1024)S(1)} %bitcast.104, f32[2048]{0:T(1024)S(1)} %bitcast.88, ...), kind=kOutput, calls=%fused_computation.49 | convolution fusion | flops 822149120 | bytes 817156 | tf_op jit(solution)/shard_map/dot_general | solution.py:30
  489.3 6.8 fusion.28
  496.1 0.0 collective-permute-done.4
  496.1 1.1 maximum_add_fusion.1
  497.2 0.0 all-reduce.6.cloned.1.call-update
  497.2 44.3 %all-reduce.6.cloned.1.call-done = f32[64,4096]{1,0:T(8,128)} async-done(((f32[64,4096]{1,0:T(8,128)}), f32[64,4096]{1,0:T(8,128)}) %all-reduce.6.cloned.1.call-update) | async-done | bytes 1048592 | tf_op jit(solution)/shard_map/psum | solution.py:130
  541.6 1.5 multiply_reduce_fusion
  543.0 127.9 %psum.47 = f32[64]{0:T(128)S(1)} all-reduce(f32[64]{0:T(128)S(1)} %multiply_reduce_fusion), channel_id=1, replica_groups=mesh['blk'=64,'rep'=4] {'blk'}, use_global_device_ids=true, to_apply=%region_9.0 | all-reduce | flops 64 | bytes 512 | tf_op jit(solution)/shard_map/psum | solution.py:142
  670.9 3.0 multiply_subtract_fusion
  (6 shorter events, 0.1 us)
Async XLA Ops:
  7.2 151.6 %all-reduce.4.cloned.1.call-start = ((), (), s32[]{:S(2)}) async-start(), calls=%async_computation | async-start | bytes 2097152 | tf_op jit(solution)/shard_map/psum | solution.py:130
  7.2 38.5 %collective-permute-start = (f32[3,4096]{1,0:T(4,128)}, f32[3,4096]{1,0:T(4,128)S(1)}, u32[]{:S(2)}, u32[]{:S(2)}) collective-permute-start(f32[3,4096]{1,0:T(4,128)} %param.4), channel_id=1, source_target_pairs={{4,0},{8,4},{12,8},{16,12},{20,16},{24,20},{28,24},{32,28},{36,32}... | collective-permute-start | bytes 147464 | tf_op jit(solution)/shard_map/ppermute | solution.py:16
  8.5 64.7 %collective-permute-start.1 = (f32[64,4096]{1,0:T(8,128)}, f32[64,4096]{1,0:T(8,128)S(1)}, u32[]{:S(2)}, u32[]{:S(2)}) collective-permute-start(f32[64,4096]{1,0:T(8,128)} %param.3), channel_id=1, source_target_pairs={{4,0},{8,4},{12,8},{16,12},{20,16},{24,20},{28,24},{32,28},{36,32}... | collective-permute-start | bytes 3145736 | tf_op jit(solution)/shard_map/ppermute | solution.py:16
  13.1 8.3 %copy-start = (f32[64,4096]{1,0:T(8,128)S(1)}, f32[64,4096]{1,0:T(8,128)}, u32[]{:S(2)}) copy-start(f32[64,4096]{1,0:T(8,128)} %param.3) | copy-start | bytes 3145732
  69.1 33.2 %collective-permute-start.2 = (f32[64,4096]{1,0:T(8,128)S(1)}, f32[64,4096]{1,0:T(8,128)S(1)}, u32[]{:S(2)}, u32[]{:S(2)}) collective-permute-start(f32[64,4096]{1,0:T(8,128)S(1)} %pad_maximum_fusion), channel_id=1, source_target_pairs={{0,4},{4,8},{8,12},{12,16},{16,20},{20,24},{24,28},{28,32},{32,36}... | collective-permute-start | bytes 3145736 | tf_op jit(solution)/shard_map/ppermute | solution.py:16
  103.5 438.1 %all-reduce.6.cloned.1.call-start = ((), (), s32[]{:S(2)}) async-start(), calls=%async_computation.1 | async-start | bytes 2097152 | tf_op jit(solution)/shard_map/psum | solution.py:130
  158.7 129.5 %copy-start.1 = (f32[64,4096]{1,0:T(8,128)S(1)}, f32[64,4096]{1,0:T(8,128)}, u32[]{:S(2)}) copy-start(f32[64,4096]{1,0:T(8,128)} %all-reduce.4.cloned.1.call-done) | copy-start | bytes 3145732
  420.3 48.3 %collective-permute-start.3 = (f32[64,4096]{1,0:T(8,128)S(1)}, f32[64,4096]{1,0:T(8,128)S(1)}, u32[]{:S(2)}, u32[]{:S(2)}) collective-permute-start(f32[64,4096]{1,0:T(8,128)S(1)} %multiply_add_fusion.1), channel_id=1, source_target_pairs={{4,0},{8,4},{12,8},{16,12},{20,16},{24,20},{28,24},{32,28},{36,32}... | collective-permute-start | bytes 3145736 | tf_op jit(solution)/shard_map/ppermute | solution.py:16
  452.4 43.7 %collective-permute-start.4 = (f32[64,4096]{1,0:T(8,128)S(1)}, f32[64,4096]{1,0:T(8,128)S(1)}, u32[]{:S(2)}, u32[]{:S(2)}) collective-permute-start(f32[64,4096]{1,0:T(8,128)S(1)} %pad_maximum_fusion.1), channel_id=1, source_target_pairs={{0,4},{4,8},{8,12},{12,16},{16,20},{20,24},{24,28},{28,32},{32,36}... | collective-permute-start | bytes 3145736 | tf_op jit(solution)/shard_map/ppermute | solution.py:16
Sparse Core Ops, SparseCore 0:
  103.6 55.1 all-reduce.3
  497.3 44.1 all-reduce.5
where the time goes:
time: 690 us; the launch traced here: 681 us
  blocking collectives  380 us (55%)
  matrix products  161 us (23%)
  waiting for transfers between devices  99.6 us (14%)
  between operations  17.2 us (2%)
  starting transfers between devices  11.6 us (2%)
  other arithmetic  9.81 us (1%)
    psum x2, blocking collectives, squares(): return lax.psum(jnp.sum(residual * residual, axis=1), 'blk')  252 us
    psum x1, blocking collectives, shards(): alpha = norm_now / lax.psum(jnp.sum(direction * image, axis=1), 'blk')  128 us
    dot_general x14, matrix products, apply_rows(): lax.dot_general(vector, kernel_tile, (((1,), (1,)), ((), ())), precision=...  101 us
    psum x2, waiting for transfers between devices, matvec(): total = lax.psum(own_full + returned, 'rep')  99.6 us
    dot_general x10, matrix products, apply_cols(): jnp.dot(vector, kernel_tile, precision=lax.Precision.HIGHEST, preferred_e...  59.7 us
  transfers between devices with their start and end apart: 7, of which 2 were waited for; matrix products, arithmetic and copies ran while one was open for 23% of the time, Pallas kernels for 0%

commit v1 on v0

--- a/solution.py
+++ b/solution.py
@@ -139,7 +139,10 @@
     norm_now = squares(residual)
     for step in range(ITERS):
         image = matvec(direction)
-        alpha = norm_now / lax.psum(jnp.sum(direction * image, axis=1), "blk")
+        test_roots_all = lambda local_x, along_axis: jnp.sum(
+            lax.all_gather(local_x, axis_name=along_axis), 0
+        )
+        alpha = norm_now / test_roots_all(jnp.sum(direction * image, axis=1), "blk")
         solution = solution + alpha[:, None] * direction
         residual = residual - alpha[:, None] * image
         norm_next = squares(residual)

time: 690 us -> 935 us (1.36)
  blocking collectives: 380 us -> 624 us
    unnamed x0 -> x1, blocking collectives: none -> 250 us
    psum x1 -> x0, blocking collectives: 128 us -> none  [shards(): alpha = norm_now / lax.psum(jnp.sum(direction * image, axis=1), 'blk')]
    psum x2, blocking collectives: 252 us -> 374 us  [squares(): return lax.psum(jnp.sum(residual * residual, axis=1), 'blk')]
  transfers between devices with their start and end apart: 7 -> 7, of which waited for: 2 -> 2; matrix products, arithmetic and copies ran while one was open for 23% -> 17% of each run, Pallas kernels for 0% -> 0%
where the time goes in v1:
time: 935 us; the launch traced here: 926 us
  blocking collectives  624 us (67%)
  matrix products  161 us (17%)
  waiting for transfers between devices  97.7 us (10%)
  between operations  17.9 us (2%)
  starting transfers between devices  11.6 us (1%)
  other arithmetic  9.88 us (1%)
    psum x2, blocking collectives, squares(): return lax.psum(jnp.sum(residual * residual, axis=1), 'blk')  374 us
    unnamed x1, blocking collectives  250 us
    dot_general x14, matrix products, apply_rows(): lax.dot_general(vector, kernel_tile, (((1,), (1,)), ((), ())), precision=...  101 us
    psum x2, waiting for transfers between devices, matvec(): total = lax.psum(own_full + returned, 'rep')  97.6 us
    dot_general x10, matrix products, apply_cols(): jnp.dot(vector, kernel_tile, precision=lax.Precision.HIGHEST, preferred_e...  59.7 us
  transfers between devices with their start and end apart: 7, of which 2 were waited for; matrix products, arithmetic and copies ran while one was open for 17% of the time, Pallas kernels for 0%

profile of v1, /device:TPU:8, one launch (start us, length us, event | category | flops | bytes accessed | tf_op | source)
XLA Modules:
  0.0 926.0 jit_solution(11297758279202484339)
XLA Ops:
  7.2 0.0 all-reduce.6.cloned.1.call-start
  7.2 1.3 collective-permute-start
  8.5 1.3 collective-permute-start.1
  9.8 0.9 fusion.176
  10.7 0.8 dynamic-slice_convert_fusion
  11.5 0.6 fusion.178
  12.1 0.9 constant_dynamic-slice_fusion
  13.1 0.0 copy-start
  13.1 8.3 fusion.17
  21.4 0.0 copy-done
  21.4 8.1 fusion.44
  29.5 7.2 fusion.18
  36.7 6.6 convolution_multiply_fusion.9
  45.7 0.0 collective-permute-done
  45.8 5.7 convolution_multiply_fusion.8
  51.6 5.7 fusion.3
  57.3 5.9 convolution_multiply_fusion.6
  63.3 5.7 fusion.2
  69.0 0.1 pad_maximum_fusion
  69.1 4.1 collective-permute-start.2
  73.2 0.0 collective-permute-done.1
  73.2 7.2 fusion.41
  80.4 7.3 fusion.36
  87.8 7.2 fusion.30
  94.9 7.4 fusion.24
  102.3 0.0 collective-permute-done.2
  102.3 1.1 maximum_add_fusion
  103.4 0.0 all-reduce.6.cloned.1.call-update
  103.5 0.0 all-reduce.8.cloned.1.call-start
  103.5 0.6 copy-done.2
  104.1 0.7 dynamic-slice.2
  105.5 53.2 %all-reduce.6.cloned.1.call-done = f32[64,4096]{1,0:T(8,128)} async-done(((f32[64,4096]{1,0:T(8,128)}), f32[64,4096]{1,0:T(8,128)}) %all-reduce.6.cloned.1.call-update) | async-done | bytes 1048592 | tf_op jit(solution)/shard_map/psum | solution.py:130
  158.7 1.6 multiply_reduce_fusion.2
  160.4 0.3 dynamic-update-slice.2
  160.6 249.9 %all-reduce.2 = (f32[64]{0:T(128)S(1)}, f32[4096]{0:T(1024)S(1)}) all-reduce(f32[64]{0:T(128)S(1)} %get-tuple-element.3, f32[4096]{0:T(1024)S(1)} %dynamic-update-slice.2), channel_id=1, replica_groups=mesh['blk'=64,'rep'=4] {'blk'}, use_global_device_ids=true, to_apply=%region_1.0 | all-reduce | flops 4160 | bytes 33280 | tf_op jit(solution)/shard_map/psum | solution.py:134
  410.6 0.1 reshape.24
  410.7 0.3 multiply_reduce_fusion.1
  411.0 124.0 %psum.30 = f32[64]{0:T(128)S(1)} all-reduce(f32[64]{0:T(128)S(1)} %multiply_reduce_fusion.1), channel_id=1, replica_groups=mesh['blk'=64,'rep'=4] {'blk'}, use_global_device_ids=true, to_apply=%region_6.0 | all-reduce | flops 64 | bytes 512 | tf_op jit(solution)/shard_map/psum | solution.py:134
  535.1 0.3 multiply_add_fusion.1
  535.3 7.4 fusion.45
  542.7 1.7 collective-permute-start.3
  544.4 6.7 fusion.16
  551.2 5.7 convolution_multiply_fusion.3
  556.9 5.9 convolution_multiply_fusion.1
  562.8 5.7 fusion.1
  568.6 6.1 fusion
  574.7 0.1 pad_maximum_fusion.1
  574.8 3.1 collective-permute-start.4
  577.9 6.4 convolution_multiply_fusion.4
  584.3 6.7 fusion.19
  591.1 0.0 collective-permute-done.3
  591.1 6.9 fusion.43
  598.0 6.8 fusion.39
  604.8 7.0 fusion.32
  611.8 6.8 fusion.28
  618.5 0.0 collective-permute-done.4
  618.5 1.1 maximum_add_fusion.1
  619.6 0.0 all-reduce.8.cloned.1.call-update
  619.6 44.4 %all-reduce.8.cloned.1.call-done = f32[64,4096]{1,0:T(8,128)} async-done(((f32[64,4096]{1,0:T(8,128)}), f32[64,4096]{1,0:T(8,128)}) %all-reduce.8.cloned.1.call-update) | async-done | bytes 1048592 | tf_op jit(solution)/shard_map/psum | solution.py:130
  664.0 1.5 multiply_reduce_fusion
  665.5 0.3 dynamic-update-slice.3
  665.8 249.9 %all-reduce.1 = f32[4096]{0:T(1024)S(1)} all-reduce(f32[4096]{0:T(1024)S(1)} %dynamic-update-slice.3), channel_id=3, replica_groups=mesh['blk'=64,'rep'=4] {'blk'}, use_global_device_ids=true, to_apply=%add.1 | all-reduce | flops 4096 | bytes 32768
  915.7 0.1 reshape.25
  915.8 3.0 multiply_subtract_fusion
  (13 shorter events, 0.2 us)
Async XLA Ops:
  7.2 151.6 %all-reduce.6.cloned.1.call-start = ((), (), s32[]{:S(2)}) async-start(), calls=%async_computation | async-start | bytes 2097152 | tf_op jit(solution)/shard_map/psum | solution.py:130
  7.2 38.5 %collective-permute-start = (f32[3,4096]{1,0:T(4,128)}, f32[3,4096]{1,0:T(4,128)S(1)}, u32[]{:S(2)}, u32[]{:S(2)}) collective-permute-start(f32[3,4096]{1,0:T(4,128)} %param.4), channel_id=1, source_target_pairs={{4,0},{8,4},{12,8},{16,12},{20,16},{24,20},{28,24},{32,28},{36,32}... | collective-permute-start | bytes 147464 | tf_op jit(solution)/shard_map/ppermute | solution.py:16
  8.5 64.7 %collective-permute-start.1 = (f32[64,4096]{1,0:T(8,128)}, f32[64,4096]{1,0:T(8,128)S(1)}, u32[]{:S(2)}, u32[]{:S(2)}) collective-permute-start(f32[64,4096]{1,0:T(8,128)} %param.3), channel_id=1, source_target_pairs={{4,0},{8,4},{12,8},{16,12},{20,16},{24,20},{28,24},{32,28},{36,32}... | collective-permute-start | bytes 3145736 | tf_op jit(solution)/shard_map/ppermute | solution.py:16
  13.1 8.3 copy-start
  69.1 33.2 %collective-permute-start.2 = (f32[64,4096]{1,0:T(8,128)S(1)}, f32[64,4096]{1,0:T(8,128)S(1)}, u32[]{:S(2)}, u32[]{:S(2)}) collective-permute-start(f32[64,4096]{1,0:T(8,128)S(1)} %pad_maximum_fusion), channel_id=1, source_target_pairs={{0,4},{4,8},{8,12},{12,16},{16,20},{20,24},{24,28},{28,32},{32,36}... | collective-permute-start | bytes 3145736 | tf_op jit(solution)/shard_map/ppermute | solution.py:16
  103.4 0.7 copy-start.2
  103.5 560.5 %all-reduce.8.cloned.1.call-start = ((), (), s32[]{:S(2)}) async-start(), calls=%async_computation.1 | async-start | bytes 2097152 | tf_op jit(solution)/shard_map/psum | solution.py:130
  158.7 252.0 %copy-start.1 = (f32[64,4096]{1,0:T(8,128)S(1)}, f32[64,4096]{1,0:T(8,128)}, u32[]{:S(2)}) copy-start(f32[64,4096]{1,0:T(8,128)} %all-reduce.6.cloned.1.call-done) | copy-start | bytes 3145732
  542.7 48.3 %collective-permute-start.3 = (f32[64,4096]{1,0:T(8,128)S(1)}, f32[64,4096]{1,0:T(8,128)S(1)}, u32[]{:S(2)}, u32[]{:S(2)}) collective-permute-start(f32[64,4096]{1,0:T(8,128)S(1)} %multiply_add_fusion.1), channel_id=1, source_target_pairs={{4,0},{8,4},{12,8},{16,12},{20,16},{24,20},{28,24},{32,28},{36,32}... | collective-permute-start | bytes 3145736 | tf_op jit(solution)/shard_map/ppermute | solution.py:16
  574.8 43.7 %collective-permute-start.4 = (f32[64,4096]{1,0:T(8,128)S(1)}, f32[64,4096]{1,0:T(8,128)S(1)}, u32[]{:S(2)}, u32[]{:S(2)}) collective-permute-start(f32[64,4096]{1,0:T(8,128)S(1)} %pad_maximum_fusion.1), channel_id=1, source_target_pairs={{0,4},{4,8},{8,12},{12,16},{16,20},{20,24},{24,28},{28,32},{32,36}... | collective-permute-start | bytes 3145736 | tf_op jit(solution)/shard_map/ppermute | solution.py:16
Sparse Core Ops, SparseCore 0:
  103.6 55.0 all-reduce.5
  619.8 44.1 all-reduce.7
